TPU v7x, 32 devices: a whole 2x2x4 slice. The times are simulated.
32 devices in a mesh: rep: 2 (over x), grp: 8 (over z, y), mem: 2 (over core).
Axes of the slice: x: 2, y: 2, z: 4, core: 2. Of those that a mesh axis runs over, the one named last changes fastest.
Arguments:
- layer_input: bfloat16 [4096, 2048], P(('rep', 'grp', 'mem')), parts along dimension 0, may hold values from -6 to 6
- output_grad: bfloat16 [4096, 2048], P(('rep', 'grp', 'mem')), parts along dimension 0, may hold values from -24 to 24
- expert_ids: int32 [4096, 8], P(('rep', 'grp', 'mem')), parts along dimension 0, may hold values from 0 to 15, all different within a row; in each aligned block of 128 rows (0 to 127, 128 to 255, ...) at most 72 rows name the same one
- route_ints: int32 [4096, 8], P(('rep', 'grp', 'mem')), parts along dimension 0, may hold values from 1 to 255
- w_gate: bfloat16 [16, 2048, 384], P(('grp', 'mem')), may hold values from -0.125 to 0.125
- w_up: bfloat16 [16, 2048, 384], P(('grp', 'mem')), may hold values from -0.125 to 0.125
- w_down: bfloat16 [16, 384, 2048], P(('grp', 'mem')), may hold values from -0.3125 to 0.3125
Outputs:
- input_grad: bfloat16 [4096, 2048], P(('rep', 'grp', 'mem')), parts along dimension 0
- grad_gate: bfloat16 [32, 2048, 384], P(('rep', 'grp', 'mem')), parts along dimension 0
- grad_up: bfloat16 [32, 2048, 384], P(('rep', 'grp', 'mem')), parts along dimension 0
- grad_down: bfloat16 [32, 384, 2048], P(('rep', 'grp', 'mem')), parts along dimension 0
There are 2 independent parts, one for each index of `rep`. A program takes and returns all parts, laid end to end along the dimension named above; an argument that names none is the same for every part. Nothing has to cross between parts.
Inputs may be any that keep to these rules, and one draw needn't show every extreme that they name: `expert_ids`: each row names 8 different experts. The 128 rows of one device name any one expert at most 72 times, and in every draw some device names some expert exactly 72 times.
All inputs are finite; a program needn't handle non-finite values.
Results may differ from a plain program's by a relative error of at most 0.0064.
Values may be sent and summed in bfloat16 or wider, within the bound.
A program may use at most 128 MiB of HBM per device.

v0:
```python
import jax
import jax.numpy as jnp
from jax import lax
from jax.sharding import PartitionSpec as P


def local(layer_input, output_grad, expert_ids, route_ints, w_gate, w_up, w_down):
    devices = lax.axis_size("grp") * lax.axis_size("mem")
    tok_rows = layer_input.shape[0]
    model_width = layer_input.shape[1]
    top_count = expert_ids.shape[1]
    pair_count = tok_rows * top_count
    capacity = max(2, 9 * tok_rows * top_count // (8 * devices))
    slot_count = devices * capacity
    quotas = route_ints.astype(jnp.float32)
    route_ratio = quotas / jnp.sum(quotas, axis=1, keepdims=True)
    scaled = (route_ratio[:, :, None] * output_grad.astype(jnp.float32)[:, None, :]).astype(
        jnp.bfloat16
    )
    scaled = scaled.reshape(pair_count, model_width)
    flat_ids = expert_ids.reshape(pair_count)
    pair_order = jnp.arange(pair_count, dtype=jnp.int32)
    earlier = (flat_ids[None, :] == flat_ids[:, None]) & (pair_order[None, :] < pair_order[:, None])
    slot_rank = jnp.sum(earlier.astype(jnp.int32), axis=1)
    slot_key = flat_ids * capacity + slot_rank
    slot_match = slot_key[None, :] == jnp.arange(slot_count, dtype=jnp.int32)[:, None]
    filled = jnp.any(slot_match, axis=1)
    source_pair = jnp.sum(jnp.where(slot_match, pair_order[None, :], 0), axis=1)
    send_x = jnp.where(
        filled[:, None], layer_input[source_pair // top_count], jnp.zeros((), jnp.bfloat16)
    )
    send_grad = jnp.where(filled[:, None], scaled[source_pair], jnp.zeros((), jnp.bfloat16))
    recv_x, recv_grad = (
        lax.all_to_all(
            send_x.reshape(devices, capacity, model_width),
            ("grp", "mem"),
            split_axis=0,
            concat_axis=0,
            tiled=True,
        ),
        lax.all_to_all(
            send_grad.reshape(devices, capacity, model_width),
            ("grp", "mem"),
            split_axis=0,
            concat_axis=0,
            tiled=True,
        ),
    )
    rows_x = recv_x.reshape(slot_count, model_width)
    rows_grad = recv_grad.reshape(slot_count, model_width)
    gate_w = w_gate[0]
    up_w = w_up[0]
    down_w = w_down[0]
    gate_pre = jnp.dot(rows_x, gate_w, preferred_element_type=jnp.float32)
    up_pre = jnp.dot(rows_x, up_w, preferred_element_type=jnp.float32)
    sigmoid_gate = jax.nn.sigmoid(gate_pre)
    activity = gate_pre * sigmoid_gate
    hidden = (activity * up_pre).astype(jnp.bfloat16)
    hidden_grad = jnp.dot(rows_grad, down_w.T, preferred_element_type=jnp.float32)
    up_grad = (hidden_grad * activity).astype(jnp.bfloat16)
    gate_grad = (
        hidden_grad * up_pre * sigmoid_gate * (1.0 + gate_pre * (1.0 - sigmoid_gate))
    ).astype(jnp.bfloat16)
    row_grad = (
        jnp.dot(gate_grad, gate_w.T, preferred_element_type=jnp.float32)
        + jnp.dot(up_grad, up_w.T, preferred_element_type=jnp.float32)
    ).astype(jnp.bfloat16)
    returned = lax.all_to_all(
        row_grad.reshape(devices, capacity, model_width),
        ("grp", "mem"),
        split_axis=0,
        concat_axis=0,
        tiled=True,
    )
    down_wgrad = jnp.dot(hidden.T, rows_grad, preferred_element_type=jnp.float32).astype(
        jnp.bfloat16
    )
    gate_wgrad = jnp.dot(rows_x.T, gate_grad, preferred_element_type=jnp.float32).astype(
        jnp.bfloat16
    )
    up_wgrad = jnp.dot(rows_x.T, up_grad, preferred_element_type=jnp.float32).astype(jnp.bfloat16)
    back_rows = returned.reshape(slot_count, model_width)
    pair_rows = back_rows[slot_key].reshape(tok_rows, top_count, model_width)
    input_grad = jnp.sum(pair_rows.astype(jnp.float32), axis=1).astype(jnp.bfloat16)
    return (input_grad, gate_wgrad[None], up_wgrad[None], down_wgrad[None])


def solution(mesh):
    return jax.shard_map(
        local,
        mesh=mesh,
        in_specs=(
            P(("rep", "grp", "mem"), None),
            P(("rep", "grp", "mem"), None),
            P(("rep", "grp", "mem"), None),
            P(("rep", "grp", "mem"), None),
            P(("grp", "mem"), None, None),
            P(("grp", "mem"), None, None),
            P(("grp", "mem"), None, None),
        ),
        out_specs=(
            P(("rep", "grp", "mem"), None),
            P(("rep", "grp", "mem"), None, None),
            P(("rep", "grp", "mem"), None, None),
            P(("rep", "grp", "mem"), None, None),
        ),
        check_vma=False,
    )
```

profile of v0, /device:TPU:15, one launch (start us, length us, event | category | flops | bytes accessed | tf_op | source)
XLA Modules:
  0.0 393.3 jit_solution(4096251935754755626)
XLA Ops:
  0.6 0.0 copy-start
  0.6 0.9 copy.14
  1.6 0.1 reshape.153
  1.6 0.5 convert_reduce_fusion
  2.2 0.6 fusion.2
  2.8 0.6 select_reduce_fusion
  3.3 0.7 convert_reduce_fusion.1
  4.1 0.7 convert_divide_fusion
  4.7 0.1 copy.15
  4.8 0.1 mul.65
  4.9 0.1 broadcast_in_dim.52
  5.0 0.1 fusion.18
  5.1 1.1 convert_element_type.38
  6.3 2.5 fusion
  8.7 0.0 copy-start.1
  8.7 13.4 %gather_fusion = bf16[1152,2048]{1,0:T(8,128)(2,1)} fusion(bf16[1024,2048]{1,0:T(8,128)(2,1)} %fusion, s32[2048]{0:T(1024)S(1)} %get-tuple-element.11), kind=kCustom, calls=%fused_computation | custom fusion | bytes 9441792 | tf_op jit(solution)/shard_map/gather | solution.py:32
  22.2 0.0 copy-done.1
  22.2 5.9 %gather_fusion.1 = bf16[1152,2048]{1,0:T(8,128)(2,1)} fusion(bf16[128,2048]{1,0:T(8,128)(2,1)S(1)} %copy-done.1, s32[2048]{0:T(1024)S(1)} %get-tuple-element.10), kind=kCustom, calls=%fused_computation.1 | custom fusion | bytes 9441792 | tf_op jit(solution)/shard_map/gather | solution.py:30
  28.1 5.6 %broadcast_select_fusion.1 = (bf16[16,72,2048]{2,1,0:T(8,128)(2,1)}, bf16[16,72,2048]{2,1,0:T(8,128)(2,1)S(1)}) fusion(bf16[16,72,2048]{2,1,0:T(8,128)(2,1)} %bitcast.45, pred[16,72]{1,0:T(8,128)(4,1)S(1)} %broadcast_in_dim.52, bf16[16,72,2048]{2,1,0:T(8,128)(2,1)} %bitcast.46), kind=kLoop, calls=%fused_computation.11 | loop fusion | flops 4718592 | bytes 18875520 | tf_op jit(solution)/shard_map/jit(_where)/select_n | solution.py:32
  33.7 109.9 %all_to_all.15 = bf16[16,72,2048]{2,1,0:T(8,128)(2,1)} all-to-all(bf16[16,72,2048]{2,1,0:T(8,128)(2,1)S(1)} %get-tuple-element.9), channel_id=1, replica_groups=mesh['rep'=2,'grp'=8,'mem'=2] {'grp','mem'}, dimensions={0} | all-to-all | bytes 9437184 | tf_op jit(solution)/shard_map/all_to_all | solution.py:34
  143.6 0.0 slice-start
  143.6 5.5 %all-to-all-start = ((bf16[16,72,2048]{2,1,0:T(8,128)(2,1)}), bf16[16,72,2048]{2,1,0:T(8,128)(2,1)}, u32[]{:S(2)}, u32[]{:S(2)}) async-start(bf16[16,72,2048]{2,1,0:T(8,128)(2,1)} %get-tuple-element.8), calls=%async_computation | async-start | bytes 9437184 | tf_op jit(solution)/shard_map/all_to_all | solution.py:41
  149.1 0.0 copy-done
  149.1 0.0 slice-start.1
  149.1 0.0 copy-start.2
  149.1 6.3 %fusion.10 = f32[1152,384]{1,0:T(8,128)} fusion(bf16[1152,2048]{1,0:T(8,128)(2,1)} %bitcast.48, bf16[1,2048,384]{2,1,0:T(8,128)(2,1)S(1)} %copy-done), kind=kOutput, calls=%fused_computation.29 | convolution fusion | flops 1811939328 | bytes 8060928 | tf_op jit(solution)/shard_map/dot_general | solution.py:54
  155.5 0.0 slice-done
  155.5 0.0 slice-done.1
  155.5 0.0 copy-done.2
  155.5 3.9 fusion.13
  159.4 93.4 %all-to-all-done = bf16[16,72,2048]{2,1,0:T(8,128)(2,1)} async-done(((bf16[16,72,2048]{2,1,0:T(8,128)(2,1)}), bf16[16,72,2048]{2,1,0:T(8,128)(2,1)}, u32[]{:S(2)}, u32[]{:S(2)}) %all-to-all-start) | async-done | bytes 4718624 | tf_op jit(solution)/shard_map/all_to_all | solution.py:41
  252.8 7.1 %multiply_convert_fusion.1 = (bf16[1152,384]{1,0:T(8,128)(2,1)S(1)}, bf16[1152,384]{1,0:T(8,128)(2,1)S(1)}) fusion(f32[1152,384]{1,0:T(8,128)} %fusion.10, f32[1152,384]{1,0:T(8,128)} %fusion.13, bf16[1152,2048]{1,0:T(8,128)(2,1)} %bitcast.2, bf16[1,384,2048]{2,1,0:T(8,128)(2,1)} %param.13), kind=kOutput, calls=%fused_computation.23 | convolution fusion | flops 1817690112 | bytes 11599872 | tf_op jit(solution)/shard_map/dot_general | solution.py:59
  259.9 0.0 copy-start.4
  259.9 0.0 copy-start.3
  259.9 2.6 fusion.8
  262.5 0.0 copy-done.4
  262.5 0.0 copy-done.3
  262.6 4.3 %fusion.1 = bf16[1152,2048]{1,0:T(8,128)(2,1)} fusion(f32[1152,2048]{1,0:T(8,128)S(1)} %fusion.8, bf16[1152,384]{1,0:T(8,128)(2,1)S(1)} %get-tuple-element.6, bf16[1,2048,384]{2,1,0:T(8,128)(2,1)S(1)} %copy-done.3), kind=kOutput, calls=%fused_computation.6 | convolution fusion | flops 1816657920 | bytes 16613376 | tf_op jit(solution)/shard_map/dot_general | solution.py:66
  266.9 0.0 copy-start.5
  266.9 0.0 slice-start.2
  266.9 5.0 %all-to-all-start.2 = ((bf16[16,72,2048]{2,1,0:T(8,128)(2,1)}), bf16[16,72,2048]{2,1,0:T(8,128)(2,1)}, u32[]{:S(2)}, u32[]{:S(2)}) async-start(bf16[16,72,2048]{2,1,0:T(8,128)(2,1)} %bitcast.47), calls=%async_computation.2 | async-start | bytes 9437184 | tf_op jit(solution)/shard_map/all_to_all | solution.py:68
  271.9 0.0 copy-done.5
  272.0 0.1 copy.16
  272.1 0.1 mul.78
  272.2 0.0 slice-start.3
  272.2 6.7 %fusion.5 = bf16[1,2048,384]{2,1,0:T(8,128)(2,1)} fusion(bf16[1152,2048]{1,0:T(8,128)(2,1)} %bitcast.49, bf16[1152,384]{1,0:T(8,128)(2,1)} %copy-done.4), kind=kOutput, calls=%fused_computation.20 | convolution fusion | flops 1812725760 | bytes 7176192 | tf_op jit(solution)/shard_map/dot_general | solution.py:81
  278.9 0.0 slice-done.2
  278.9 0.0 slice-done.3
  278.9 0.0 copy-start.6
  278.9 0.0 copy-start.7
  278.9 3.9 fusion.4
  282.8 0.0 copy-done.6
  282.8 0.0 copy-done.7
  282.9 5.9 %fusion.6 = bf16[1,384,2048]{2,1,0:T(8,128)(2,1)} fusion(bf16[1152,2048]{1,0:T(8,128)(2,1)} %bitcast.2, f32[1152,384]{1,0:T(8,128)S(1)} %copy-done.7, f32[1152,384]{1,0:T(8,128)S(1)} %copy-done.6), kind=kOutput, calls=%fused_computation.21 | convolution fusion | flops 1815379968 | bytes 9830400 | tf_op jit(solution)/shard_map/dot_general | solution.py:75
  288.7 86.9 %all-to-all-done.2 = bf16[16,72,2048]{2,1,0:T(8,128)(2,1)} async-done(((bf16[16,72,2048]{2,1,0:T(8,128)(2,1)}), bf16[16,72,2048]{2,1,0:T(8,128)(2,1)}, u32[]{:S(2)}, u32[]{:S(2)}) %all-to-all-start.2) | async-done | bytes 4718624 | tf_op jit(solution)/shard_map/all_to_all | solution.py:68
  375.7 11.8 %gather_fusion.2 = bf16[1024,2048]{1,0:T(8,128)(2,1)} fusion(bf16[1152,2048]{1,0:T(8,128)(2,1)} %bitcast.9, s32[1024]{0:T(1024)S(1)} %broadcast_clamp_fusion), kind=kCustom, calls=%fused_computation.2 | custom fusion | bytes 8392704 | tf_op jit(solution)/shard_map/gather | solution.py:83
  387.4 5.9 %bitcast_reduce_fusion = bf16[128,2048]{1,0:T(8,128)(2,1)} fusion(bf16[1024,2048]{1,0:T(8,128)(2,1)} %gather_fusion.2), kind=kLoop, calls=%fused_computation.12 | loop fusion | flops 1835008 | bytes 4718592 | tf_op jit(solution)/shard_map/reduce_sum | solution.py:84
  (7 shorter events, 0.0 us)
Async XLA Ops:
  0.6 148.5 %copy-start = (bf16[1,2048,384]{2,1,0:T(8,128)(2,1)S(1)}, bf16[1,2048,384]{2,1,0:T(8,128)(2,1)}, u32[]{:S(2)}) copy-start(bf16[1,2048,384]{2,1,0:T(8,128)(2,1)} %param.11) | copy-start | bytes 4718596
  8.7 13.5 %copy-start.1 = (bf16[128,2048]{1,0:T(8,128)(2,1)S(1)}, bf16[128,2048]{1,0:T(8,128)(2,1)}, u32[]{:S(2)}) copy-start(bf16[128,2048]{1,0:T(8,128)(2,1)} %param.7) | copy-start | bytes 1572868
  143.6 11.9 %slice-start = ((s8[4718592]{0:T(1024)(128)(4,1)}), s8[524288]{0:T(1024)(128)(4,1)S(1)}, s32[]{:S(2)}) async-start(s8[4718592]{0:T(1024)(128)(4,1)} %bitcast.50), calls=%async_computation.3 | async-start | bytes 1048576
  143.6 109.2 %all-to-all-start = ((bf16[16,72,2048]{2,1,0:T(8,128)(2,1)}), bf16[16,72,2048]{2,1,0:T(8,128)(2,1)}, u32[]{:S(2)}, u32[]{:S(2)}) async-start(bf16[16,72,2048]{2,1,0:T(8,128)(2,1)} %get-tuple-element.8), calls=%async_computation | async-start | bytes 9437184 | tf_op jit(solution)/shard_map/all_to_all | solution.py:41
  149.1 6.4 %slice-start.1 = ((s8[4718592]{0:T(1024)(128)(4,1)}), s8[4194304]{0:T(1024)(128)(4,1)S(1)}, s32[]{:S(2)}) async-start(s8[4718592]{0:T(1024)(128)(4,1)} %bitcast.50), calls=%async_computation.4 | async-start | bytes 8388608
  149.1 6.4 %copy-start.2 = (bf16[1,2048,384]{2,1,0:T(8,128)(2,1)S(1)}, bf16[1,2048,384]{2,1,0:T(8,128)(2,1)}, u32[]{:S(2)}) copy-start(bf16[1,2048,384]{2,1,0:T(8,128)(2,1)} %param.12) | copy-start | bytes 4718596
  259.9 2.7 copy-start.4
  259.9 2.7 copy-start.3
  266.9 5.0 %copy-start.5 = (s32[128,8]{0,1:T(8,128)S(1)}, s32[128,8]{0,1:T(8,128)}, u32[]{:S(2)}) copy-start(s32[128,8]{0,1:T(8,128)} %param.9) | copy-start | bytes 12292
  266.9 12.0 %slice-start.2 = ((s8[4718592]{0:T(1024)(128)(4,1)}), s8[524288]{0:T(1024)(128)(4,1)S(1)}, s32[]{:S(2)}) async-start(s8[4718592]{0:T(1024)(128)(4,1)} %bitcast.53), calls=%async_computation.5 | async-start | bytes 1048576
  266.9 108.7 %all-to-all-start.2 = ((bf16[16,72,2048]{2,1,0:T(8,128)(2,1)}), bf16[16,72,2048]{2,1,0:T(8,128)(2,1)}, u32[]{:S(2)}, u32[]{:S(2)}) async-start(bf16[16,72,2048]{2,1,0:T(8,128)(2,1)} %bitcast.47), calls=%async_computation.2 | async-start | bytes 9437184 | tf_op jit(solution)/shard_map/all_to_all | solution.py:68
  272.2 6.7 %slice-start.3 = ((s8[4718592]{0:T(1024)(128)(4,1)}), s8[4194304]{0:T(1024)(128)(4,1)S(1)}, s32[]{:S(2)}) async-start(s8[4718592]{0:T(1024)(128)(4,1)} %bitcast.53), calls=%async_computation.6 | async-start | bytes 8388608
  278.9 3.9 %copy-start.6 = (f32[1152,384]{1,0:T(8,128)S(1)}, f32[1152,384]{1,0:T(8,128)}, u32[]{:S(2)}) copy-start(f32[1152,384]{1,0:T(8,128)} %fusion.10) | copy-start | bytes 5308420
  278.9 3.9 copy-start.7
where the time goes:
time: 394 us; the launch traced here: 393 us
  waiting for transfers between devices  180 us (46%)
  blocking collectives  110 us (28%)
  matrix products  40.7 us (10%)
  local copies, waits for them, and re-layouts  32.6 us (8%)
  other arithmetic  18.3 us (5%)
  starting transfers between devices  10.5 us (3%)
    all_to_all x1, blocking collectives, local(): lax.all_to_all(send_x.reshape(devices, capacity, model_width), ('grp', 'm...  110 us
    all_to_all x1, waiting for transfers between devices, local(): lax.all_to_all(send_grad.reshape(devices, capacity, model_width), ('grp',...  93.4 us
    all_to_all x1, waiting for transfers between devices, local(): lax.all_to_all(row_grad.reshape(devices, capacity, model_width), ('grp',...  86.9 us
    gather x1, local copies, waits for them, and re-layouts, local(): scaled[source_pair]  13.4 us
    gather x1, local copies, waits for them, and re-layouts, local(): pair_rows = back_rows[slot_key].reshape(tok_rows, top_count, model_width)  11.8 us
  transfers between devices with their start and end apart: 2, of which 2 were waited for; matrix products, arithmetic and copies ran while one was open for 7% of the time, Pallas kernels for 0%

commit v1 on v0

--- a/solution.py
+++ b/solution.py
@@ -1,10 +1,12 @@
 import jax
 import jax.numpy as jnp
 from jax import lax
+from jax.experimental import pallas as pl
+from jax.experimental.pallas import tpu as pltpu
 from jax.sharding import PartitionSpec as P
 
 
-def local(layer_input, output_grad, expert_ids, route_ints, w_gate, w_up, w_down):
+def routed(layer_input, output_grad, expert_ids, route_ints, w_gate, w_up, w_down):
     devices = lax.axis_size("grp") * lax.axis_size("mem")
     tok_rows = layer_input.shape[0]
     model_width = layer_input.shape[1]
@@ -84,6 +86,380 @@
     input_grad = jnp.sum(pair_rows.astype(jnp.float32), axis=1).astype(jnp.bfloat16)
     return (input_grad, gate_wgrad[None], up_wgrad[None], down_wgrad[None])
 
+F32 = jnp.float32
+BF16 = jnp.bfloat16
+MESH = pl.DeviceIdType.MESH
+UP, DOWN, ACROSS, BESIDE = 0, 1, 2, 3
+
+
+def dense_kernel(
+    x_hbm, g_hbm, s_hbm, gw_hbm, uw_hbm, dw_hbm,
+    ig_ref, gg_ref, ug_ref, dg_ref,
+    xs, gs, ss, w, wd, gu, ht, rc, rp, rb, ra, ru, rd,
+    load_sem, send_sem, recv_sem, rb_send, rb_recv, ra_send, ra_recv, ru_send, ru_recv,
+    rd_send, rd_recv,
+):
+    rep, grp, mem = lax.axis_index("rep"), lax.axis_index("grp"), lax.axis_index("mem")
+    groups = lax.axis_size("grp")
+    cores = lax.axis_size("mem")
+    rows = x_hbm.shape[0]
+    width = x_hbm.shape[1]
+    ff = gw_hbm.shape[1]
+    experts = s_hbm.shape[0]
+    length = groups // 2
+    z, y = grp // 2, grp % 2
+    me = grp * cores + mem
+    peers = {
+        UP: (rep, (z + 1) * 2 + y, mem),
+        DOWN: (rep, (z - 1) * 2 + y, mem),
+        ACROSS: (rep, z * 2 + 1 - y, mem),
+        BESIDE: (rep, grp, 1 - mem),
+    }
+    has_up, has_down = z < length - 1, z > 0
+
+    def slot(g, c, size):
+        return pl.ds(pl.multiple_of((g * cores + c) * size, size), size)
+
+    sizes = (rows, rows, experts)
+    bufs = (xs, gs, ss)
+    loads = [
+        pltpu.make_async_copy(h, b.at[slot(grp, mem, n)], load_sem.at[i])
+        for i, (h, b, n) in enumerate(zip((x_hbm, g_hbm, s_hbm), bufs, sizes))
+    ]
+    loads.append(pltpu.make_async_copy(gw_hbm, w.at[:, pl.ds(0, ff)], load_sem.at[3]))
+    loads.append(pltpu.make_async_copy(uw_hbm, w.at[:, pl.ds(ff, ff)], load_sem.at[4]))
+    loads.append(pltpu.make_async_copy(dw_hbm, wd, load_sem.at[5]))
+    for load in loads:
+        load.start()
+
+    barrier = pltpu.get_barrier_semaphore()
+    for way, there in ((UP, has_up), (DOWN, has_down), (ACROSS, None), (BESIDE, None)):
+
+        def hail(way=way):
+            pl.semaphore_signal(barrier, inc=1, device_id=peers[way], device_id_type=MESH)
+
+        hail() if there is None else pl.when(there)(hail)
+    pl.semaphore_wait(barrier, 2 + jnp.where(has_up, 1, 0) + jnp.where(has_down, 1, 0))
+
+    for load in loads[:3]:
+        load.wait()
+
+    def hop(way, a, g, c):
+        ref = bufs[a].at[slot(g, c, sizes[a])]
+        return pltpu.make_async_remote_copy(
+            src_ref=ref,
+            dst_ref=ref,
+            send_sem=send_sem.at[way, a, g],
+            recv_sem=recv_sem.at[a, g * cores + c],
+            device_id=peers[way],
+            device_id_type=MESH,
+        )
+
+    def beside(g):
+        return pltpu.make_async_remote_copy(
+            src_ref=rp.at[slot(g, 1 - mem, rows)],
+            dst_ref=rb.at[pl.ds(pl.multiple_of(g * rows, rows), rows)],
+            send_sem=rb_send.at[g],
+            recv_sem=rb_recv.at[g],
+            device_id=peers[BESIDE],
+            device_id_type=MESH,
+        )
+
+    def line(way, d):
+        buf, snd, rcv = {
+            UP: (ru, ru_send, ru_recv),
+            DOWN: (rd, rd_send, rd_recv),
+            ACROSS: (ra, ra_send, ra_recv),
+        }[way]
+        row = 1 - y if way == ACROSS else y
+        return pltpu.make_async_remote_copy(
+            src_ref=rp.at[slot(d * 2 + row, mem, rows)],
+            dst_ref=buf.at[pl.ds(pl.multiple_of(d * rows, rows), rows)],
+            send_sem=snd.at[d],
+            recv_sem=rcv.at[d],
+            device_id=peers[way],
+            device_id_type=MESH,
+        )
+
+    def add_into(g, buf, b):
+        step = 16
+
+        @pl.loop(0, rows // step)
+        def _(i):
+            at = pl.ds(pl.multiple_of((g * cores + mem) * rows + i * step, step), step)
+            other = pl.ds(pl.multiple_of(b * rows + i * step, step), step)
+            rp[at, :] = (rp[at, :].astype(F32) + buf[other, :].astype(F32)).astype(BF16)
+
+    def place(q):
+        s = (q + 1) // 2
+        sign = 1 - 2 * (q % 2)
+        oz = z + sign * s
+        return oz, (q >= 0) & (q < 2 * length - 1) & (oz >= 0) & (oz < length)
+
+    def along(p):
+        oz, valid = place(p)
+        g = oz * 2 + y
+
+        @pl.when(valid)
+        def _():
+            for a in (2, 0, 1):
+
+                @pl.when(p > 0)
+                def _():
+                    hop(UP, a, g, mem).wait_recv()
+
+                @pl.when((oz <= z) & has_up)
+                def _():
+                    hop(UP, a, g, mem).start()
+
+                @pl.when((oz >= z) & has_down)
+                def _():
+                    hop(DOWN, a, g, mem).start()
+
+                hop(ACROSS, a, g, mem).start()
+                hop(BESIDE, a, g, mem).start()
+
+    def across(q):
+        oz, valid = place(q)
+        g = oz * 2 + 1 - y
+
+        @pl.when(valid)
+        def _():
+            for a in (2, 0, 1):
+                hop(ACROSS, a, g, mem).wait_recv()
+                hop(BESIDE, a, g, mem).start()
+
+    def merge(q, row):
+        oz, valid = place(q)
+        g = oz * 2 + row
+
+        @pl.when(valid)
+        def _():
+            beside(g).wait_recv()
+            add_into(g, rb, g)
+
+            @pl.when(row != y)
+            def _():
+                line(ACROSS, oz).start()
+
+    def chunk(g):
+        for a in (2, 0, 1):
+            hop(BESIDE, a, g, 1 - mem).wait_recv()
+        block = pl.ds(pl.multiple_of(g * cores * rows, cores * rows), cores * rows)
+        ratios = []
+        for c in range(cores):
+            share = ss[slot(g, c, experts), :]
+            picked = lax.broadcasted_iota(jnp.int32, share.shape, 0) == me
+            row = jnp.sum(jnp.where(picked, share, 0.0), axis=0, keepdims=True)
+            square = jnp.broadcast_to(row, (rows, rows))
+            diagonal = lax.broadcasted_iota(jnp.int32, (rows, rows), 0) == (
+                lax.broadcasted_iota(jnp.int32, (rows, rows), 1)
+            )
+            ratios.append(jnp.sum(jnp.where(diagonal, square, 0.0), axis=1, keepdims=True))
+        ratio = jnp.concatenate(ratios, axis=0)
+        rc[block, :] = ratio
+        pre = jnp.dot(xs[block, :], w[...], preferred_element_type=F32)
+        gate_pre, up_pre = pre[:, :ff], pre[:, ff:]
+        sg = (ratio * gs[block, :].astype(F32)).astype(BF16)
+        hidden_grad = lax.dot_general(
+            sg, wd[...], (((1,), (1,)), ((), ())), preferred_element_type=F32
+        )
+        sig = jax.nn.sigmoid(gate_pre)
+        act = gate_pre * sig
+        ht[:, block] = (act * up_pre).T.astype(BF16)
+        gate_grad = (hidden_grad * up_pre * sig * (1.0 + gate_pre * (1.0 - sig))).astype(BF16)
+        up_grad = (hidden_grad * act).astype(BF16)
+        gu[block, pl.ds(0, ff)] = gate_grad
+        gu[block, pl.ds(ff, ff)] = up_grad
+        both = jnp.concatenate([gate_grad, up_grad], axis=1)
+        rp[block, :] = lax.dot_general(
+            both, w[...], (((1,), (1,)), ((), ())), preferred_element_type=F32
+        ).astype(BF16)
+        beside(g).start()
+
+    @pl.loop(0, 2 * length + 1)
+    def _(p):
+        along(p)
+        across(p - 1)
+
+        @pl.when(p == 0)
+        def _():
+            for load in loads[3:]:
+                load.wait()
+
+        @pl.loop(0, 2)
+        def _(j):
+            merge(p - 2 + j, jnp.where(j == 0, 1 - y, y))
+
+        @pl.loop(0, 2)
+        def _(j):
+            oz, valid = place(p - 1 + j)
+
+            @pl.when(valid)
+            def _():
+                chunk(oz * 2 + jnp.where(j == 0, 1 - y, y))
+
+    def gather_across(d):
+        line(ACROSS, d).wait_recv()
+        add_into(d * 2 + y, ra, d)
+
+    tile = width // (2 * length)
+
+    @pl.loop(0, length)
+    def _(i):
+        d = length - 1 - i
+
+        @pl.when(d > z)
+        def _():
+            gather_across(d)
+
+            @pl.when(has_down)
+            def _():
+                line(UP, d).wait_recv()
+                add_into(d * 2 + y, ru, d)
+
+            line(UP, d).start()
+
+        @pl.when(i < z)
+        def _():
+            gather_across(i)
+
+            @pl.when(has_up)
+            def _():
+                line(DOWN, i).wait_recv()
+                add_into(i * 2 + y, rd, i)
+
+            line(DOWN, i).start()
+
+        @pl.loop(0, 2)
+        def _(t):
+            cols = pl.ds(pl.multiple_of((i * 2 + t) * tile, tile), tile)
+            wide = lax.dot_general(
+                xs[:, cols], gu[...], (((0,), (0,)), ((), ())), preferred_element_type=F32
+            ).astype(BF16)
+            gg_ref[cols, :] = wide[:, :ff]
+            ug_ref[cols, :] = wide[:, ff:]
+            sg = (rc[...] * gs[:, cols].astype(F32)).astype(BF16)
+            dg_ref[:, cols] = jnp.dot(ht[...], sg, preferred_element_type=F32).astype(BF16)
+
+    gather_across(z)
+
+    @pl.when(has_down)
+    def _():
+        line(UP, z).wait_recv()
+        add_into(grp, ru, z)
+
+    @pl.when(has_up)
+    def _():
+        line(DOWN, z).wait_recv()
+        add_into(grp, rd, z)
+
+    ig_ref[...] = rp[slot(grp, mem, rows), :]
+
+    @pl.loop(0, groups)
+    def _(g):
+        for a in range(3):
+            hop(BESIDE, a, g, mem).wait_send()
+        beside(g).wait_send()
+
+    @pl.loop(0, length)
+    def _(d):
+        g = d * 2 + y
+        for a in range(3):
+            hop(ACROSS, a, g, mem).wait_send()
+
+            @pl.when((d <= z) & has_up)
+            def _():
+                hop(UP, a, g, mem).wait_send()
+
+            @pl.when((d >= z) & has_down)
+            def _():
+                hop(DOWN, a, g, mem).wait_send()
+
+        line(ACROSS, d).wait_send()
+
+        @pl.when(d > z)
+        def _():
+            line(UP, d).wait_send()
+
+        @pl.when(d < z)
+        def _():
+            line(DOWN, d).wait_send()
+
+
+def dense(layer_input, output_grad, expert_ids, route_ints, w_gate, w_up, w_down):
+    groups, cores = lax.axis_size("grp"), lax.axis_size("mem")
+    devices = groups * cores
+    length = groups // 2
+    tok_rows, width = layer_input.shape
+    ff = w_gate.shape[2]
+    total = devices * tok_rows
+    quotas = route_ints.astype(F32)
+    route_ratio = quotas / jnp.sum(quotas, axis=1, keepdims=True)
+    experts = jnp.arange(devices, dtype=jnp.int32)
+    share = jnp.sum(
+        jnp.where(
+            expert_ids.T[None, :, :] == experts[:, None, None], route_ratio.T[None, :, :], 0.0
+        ),
+        axis=1,
+    )
+    dma = pltpu.SemaphoreType.DMA
+    outs = pl.pallas_call(
+        dense_kernel,
+        out_shape=(
+            jax.ShapeDtypeStruct((tok_rows, width), BF16),
+            jax.ShapeDtypeStruct((width, ff), BF16),
+            jax.ShapeDtypeStruct((width, ff), BF16),
+            jax.ShapeDtypeStruct((ff, width), BF16),
+        ),
+        in_specs=[pl.BlockSpec(memory_space=pl.ANY)] * 6,
+        out_specs=tuple([pl.BlockSpec(memory_space=pltpu.VMEM)] * 4),
+        scratch_shapes=[
+            pltpu.VMEM((total, width), BF16),
+            pltpu.VMEM((total, width), BF16),
+            pltpu.VMEM((devices * devices, tok_rows), F32),
+            pltpu.VMEM((width, 2 * ff), BF16),
+            pltpu.VMEM((ff, width), BF16),
+            pltpu.VMEM((total, 2 * ff), BF16),
+            pltpu.VMEM((ff, total), BF16),
+            pltpu.VMEM((total, 1), F32),
+            pltpu.VMEM((total, width), BF16),
+            pltpu.VMEM((groups * tok_rows, width), BF16),
+            pltpu.VMEM((length * tok_rows, width), BF16),
+            pltpu.VMEM((length * tok_rows, width), BF16),
+            pltpu.VMEM((length * tok_rows, width), BF16),
+            dma((6,)),
+            dma((4, 3, groups)),
+            dma((3, devices)),
+            dma((groups,)),
+            dma((groups,)),
+            dma((length,)),
+            dma((length,)),
+            dma((length,)),
+            dma((length,)),
+            dma((length,)),
+            dma((length,)),
+        ],
+        compiler_params=pltpu.CompilerParams(
+            collective_id=0, has_side_effects=True, vmem_limit_bytes=60 * 1024 * 1024
+        ),
+        cost_estimate=pl.CostEstimate(
+            flops=16 * total * width * ff,
+            bytes_accessed=12 * width * ff + 6 * tok_rows * width,
+            transcendentals=total * ff,
+        ),
+    )(layer_input, output_grad, share, w_gate[0], w_up[0], w_down[0])
+    return (outs[0], outs[1][None], outs[2][None], outs[3][None])
+
+
+def local(layer_input, output_grad, expert_ids, *rest):
+    groups, cores = lax.axis_size("grp"), lax.axis_size("mem")
+    tok_rows, top_count = expert_ids.shape
+    capacity = max(2, 9 * tok_rows * top_count // (8 * groups * cores))
+    suits = tok_rows <= 2 * capacity and groups % 2 == 0 and cores == 2
+    plan = dense if suits else routed
+    return plan(layer_input, output_grad, expert_ids, *rest)
+
 
 def solution(mesh):
     return jax.shard_map(

time: 394 us -> 214 us (0.54)
  the two profiles are of different devices: /device:TPU:15 before, /device:TPU:0 now
where the time goes in v1:
time: 214 us; the launch traced here: 213 us
  Pallas kernels  202 us (94%)
  local copies, waits for them, and re-layouts  7.83 us (4%)
  other arithmetic  2.7 us (1%)
    pallas_call x1, Pallas kernels, dense(): pl.pallas_call(dense_kernel, out_shape=(jax.ShapeDtypeStruct((tok_rows, w...  202 us
    unnamed x8, local copies, waits for them, and re-layouts  7.83 us

profile of v1, /device:TPU:0, one launch (start us, length us, event | category | flops | bytes accessed | tf_op | source)
XLA Modules:
  0.0 213.1 jit_solution(659287784939128912)
XLA Ops:
  0.6 0.7 convert_reduce_fusion
  1.3 0.7 divide_bitcast_fusion
  2.0 1.3 select_reduce_fusion.s_hbm
  3.3 202.0 %shard_map.102 = (bf16[128,2048]{1,0:T(8,128)(2,1)}, bf16[2048,384]{1,0:T(8,128)(2,1)}, bf16[2048,384]{1,0:T(8,128)(2,1)}, bf16[384,2048]{1,0:T(8,128)(2,1)}) custom-call(bf16[128,2048]{1,0:T(8,128)(2,1)} %x_hbm.1, bf16[128,2048]{1,0:T(8,128)(2,1)} %g_hbm.1, f32[16,128]{1,0:T(8,128)} %select_reduce_fusion.s_hbm, bf16[2048,384]{1,0:T(8,128)(2,1)} %bitcast.13, ...), custom_call_target="tpu_custom_call" | custom-call | flops 25769803776 | bytes 11010048 | tf_op jit(solution)/shard_map/pallas_call | solution.py:407
  205.3 1.9 copy.15
  207.2 0.0 copy-start.1
  207.2 2.8 %copy.16 = bf16[1,2048,384]{2,1,0:T(8,128)(2,1)} copy(bf16[1,2048,384]{2,1,0:T(8,128)(2,1)} %bitcast.11) | data formatting | bytes 3145728
  210.0 0.0 copy-done.1
  210.0 0.0 copy-start
  210.0 1.1 copy.17
  211.2 0.8 copy-done
  212.0 1.1 copy.18
Async XLA Ops:
  207.2 2.8 %copy-start.1 = (bf16[2048,384]{1,0:T(8,128)(2,1)S(1)}, bf16[2048,384]{1,0:T(8,128)(2,1)}, u32[]{:S(2)}) copy-start(bf16[2048,384]{1,0:T(8,128)(2,1)} %get-tuple-element.10) | copy-start | bytes 4718596
  210.0 2.0 copy-start

commit v2 on v1

--- a/solution.py
+++ b/solution.py
@@ -165,29 +165,32 @@
             device_id_type=MESH,
         )
 
-    def line(way, d):
+    half = rows // 2
+
+    def line(way, g, h):
         buf, snd, rcv = {
             UP: (ru, ru_send, ru_recv),
             DOWN: (rd, rd_send, rd_recv),
             ACROSS: (ra, ra_send, ra_recv),
         }[way]
-        row = 1 - y if way == ACROSS else y
+        at = 0 if way == ACROSS else g
         return pltpu.make_async_remote_copy(
-            src_ref=rp.at[slot(d * 2 + row, mem, rows)],
-            dst_ref=buf.at[pl.ds(pl.multiple_of(d * rows, rows), rows)],
-            send_sem=snd.at[d],
-            recv_sem=rcv.at[d],
+            src_ref=rp.at[pl.ds(pl.multiple_of((g * cores + mem) * rows + h * half, half), half)],
+            dst_ref=buf.at[pl.ds(pl.multiple_of(at * rows + h * half, half), half)],
+            send_sem=snd.at[at, h],
+            recv_sem=rcv.at[at, h],
             device_id=peers[way],
             device_id_type=MESH,
         )
 
-    def add_into(g, buf, b):
+    def add_into(g, buf, b, h):
         step = 16
 
-        @pl.loop(0, rows // step)
+        @pl.loop(0, half // step)
         def _(i):
-            at = pl.ds(pl.multiple_of((g * cores + mem) * rows + i * step, step), step)
-            other = pl.ds(pl.multiple_of(b * rows + i * step, step), step)
+            shift = h * half + i * step
+            at = pl.ds(pl.multiple_of((g * cores + mem) * rows + shift, step), step)
+            other = pl.ds(pl.multiple_of(b * rows + shift, step), step)
             rp[at, :] = (rp[at, :].astype(F32) + buf[other, :].astype(F32)).astype(BF16)
 
     def place(q):
@@ -196,13 +199,13 @@
         oz = z + sign * s
         return oz, (q >= 0) & (q < 2 * length - 1) & (oz >= 0) & (oz < length)
 
-    def along(p):
+    def along(p, arrays):
         oz, valid = place(p)
         g = oz * 2 + y
 
         @pl.when(valid)
         def _():
-            for a in (2, 0, 1):
+            for a in arrays:
 
                 @pl.when(p > 0)
                 def _():
@@ -236,11 +239,18 @@
         @pl.when(valid)
         def _():
             beside(g).wait_recv()
-            add_into(g, rb, g)
-
-            @pl.when(row != y)
-            def _():
-                line(ACROSS, oz).start()
+
+            @pl.loop(0, 2)
+            def _(h):
+                add_into(g, rb, g, h)
+
+                @pl.when((oz > z) & ~has_down)
+                def _():
+                    line(UP, g, h).start()
+
+                @pl.when((oz < z) & ~has_up)
+                def _():
+                    line(DOWN, g, h).start()
 
     def chunk(g):
         for a in (2, 0, 1):
@@ -277,63 +287,70 @@
         ).astype(BF16)
         beside(g).start()
 
+    def ahead(p, arrays):
+        @pl.loop(0, 2)
+        def _(k):
+            @pl.when((p % 2 == 1) | (p + k == 0))
+            def _():
+                along(p + k, arrays)
+
     @pl.loop(0, 2 * length + 1)
     def _(p):
-        along(p)
-        across(p - 1)
-
-        @pl.when(p == 0)
-        def _():
-            for load in loads[3:]:
-                load.wait()
-
         @pl.loop(0, 2)
         def _(j):
-            merge(p - 2 + j, jnp.where(j == 0, 1 - y, y))
-
-        @pl.loop(0, 2)
-        def _(j):
+            @pl.when(j == 0)
+            def _():
+                ahead(p, (2, 0))
+                across(p - 1)
+
+                @pl.loop(0, 2)
+                def _(k):
+                    merge(p - 2 + k, jnp.where(k == 0, 1 - y, y))
+
+            @pl.when(j == 1)
+            def _():
+                ahead(p, (1,))
+
+                @pl.when(p == 0)
+                def _():
+                    for load in loads[3:]:
+                        load.wait()
+
             oz, valid = place(p - 1 + j)
 
             @pl.when(valid)
             def _():
                 chunk(oz * 2 + jnp.where(j == 0, 1 - y, y))
 
-    def gather_across(d):
-        line(ACROSS, d).wait_recv()
-        add_into(d * 2 + y, ra, d)
+    def relay(level, near):
+        up, down = near, length - 1 - near
+
+        @pl.loop(0, 4)
+        def _(k):
+            row = jnp.where(k < 2, y, 1 - y)
+            h = k % 2
+
+            @pl.when((z == level) & (up > z))
+            def _():
+                g = up * 2 + row
+                line(UP, g, h).wait_recv()
+                add_into(g, ru, g, h)
+                line(UP, g, h).start()
+
+            @pl.when((length - 1 - z == level) & (down < z))
+            def _():
+                g = down * 2 + row
+                line(DOWN, g, h).wait_recv()
+                add_into(g, rd, g, h)
+                line(DOWN, g, h).start()
 
     tile = width // (2 * length)
 
-    @pl.loop(0, length)
-    def _(i):
-        d = length - 1 - i
-
-        @pl.when(d > z)
-        def _():
-            gather_across(d)
-
-            @pl.when(has_down)
-            def _():
-                line(UP, d).wait_recv()
-                add_into(d * 2 + y, ru, d)
-
-            line(UP, d).start()
-
-        @pl.when(i < z)
-        def _():
-            gather_across(i)
-
-            @pl.when(has_up)
-            def _():
-                line(DOWN, i).wait_recv()
-                add_into(i * 2 + y, rd, i)
-
-            line(DOWN, i).start()
-
-        @pl.loop(0, 2)
-        def _(t):
-            cols = pl.ds(pl.multiple_of((i * 2 + t) * tile, tile), tile)
+    @pl.loop(0, max(2 * length, (length - 1) * length))
+    def _(t):
+        @pl.when(t < 2 * length)
+        def _():
+            cols = pl.ds(pl.multiple_of(t * tile, tile), tile)
             wide = lax.dot_general(
                 xs[:, cols], gu[...], (((0,), (0,)), ((), ())), preferred_element_type=F32
             ).astype(BF16)
@@ -342,17 +359,31 @@
             sg = (rc[...] * gs[:, cols].astype(F32)).astype(BF16)
             dg_ref[:, cols] = jnp.dot(ht[...], sg, preferred_element_type=F32).astype(BF16)
 
-    gather_across(z)
-
-    @pl.when(has_down)
-    def _():
-        line(UP, z).wait_recv()
-        add_into(grp, ru, z)
-
-    @pl.when(has_up)
-    def _():
-        line(DOWN, z).wait_recv()
-        add_into(grp, rd, z)
+        relay(1 + t // length, t % length)
+
+    @pl.loop(0, 4)
+    def _(k):
+        g = z * 2 + jnp.where(k < 2, 1 - y, y)
+        h = k % 2
+
+        @pl.when(has_down)
+        def _():
+            line(UP, g, h).wait_recv()
+            add_into(g, ru, g, h)
+
+        @pl.when(has_up)
+        def _():
+            line(DOWN, g, h).wait_recv()
+            add_into(g, rd, g, h)
+
+        @pl.when(k < 2)
+        def _():
+            line(ACROSS, g, h).start()
+
+    @pl.loop(0, 2)
+    def _(h):
+        line(ACROSS, grp, h).wait_recv()
+        add_into(grp, ra, 0, h)
 
     ig_ref[...] = rp[slot(grp, mem, rows), :]
 
@@ -376,15 +407,19 @@
             def _():
                 hop(DOWN, a, g, mem).wait_send()
 
-        line(ACROSS, d).wait_send()
-
-        @pl.when(d > z)
-        def _():
-            line(UP, d).wait_send()
-
-        @pl.when(d < z)
-        def _():
-            line(DOWN, d).wait_send()
+        @pl.loop(0, 4)
+        def _(k):
+            @pl.when(d > z)
+            def _():
+                line(UP, d * 2 + k // 2, k % 2).wait_send()
+
+            @pl.when(d < z)
+            def _():
+                line(DOWN, d * 2 + k // 2, k % 2).wait_send()
+
+    @pl.loop(0, 2)
+    def _(h):
+        line(ACROSS, z * 2 + 1 - y, h).wait_send()
 
 
 def dense(layer_input, output_grad, expert_ids, route_ints, w_gate, w_up, w_down):
@@ -425,20 +460,20 @@
             pltpu.VMEM((total, 1), F32),
             pltpu.VMEM((total, width), BF16),
             pltpu.VMEM((groups * tok_rows, width), BF16),
-            pltpu.VMEM((length * tok_rows, width), BF16),
-            pltpu.VMEM((length * tok_rows, width), BF16),
-            pltpu.VMEM((length * tok_rows, width), BF16),
+            pltpu.VMEM((tok_rows, width), BF16),
+            pltpu.VMEM((groups * tok_rows, width), BF16),
+            pltpu.VMEM((groups * tok_rows, width), BF16),
             dma((6,)),
             dma((4, 3, groups)),
             dma((3, devices)),
             dma((groups,)),
             dma((groups,)),
-            dma((length,)),
-            dma((length,)),
-            dma((length,)),
-            dma((length,)),
-            dma((length,)),
-            dma((length,)),
+            dma((1, 2)),
+            dma((1, 2)),
+            dma((groups, 2)),
+            dma((groups, 2)),
+            dma((groups, 2)),
+            dma((groups, 2)),
         ],
         compiler_params=pltpu.CompilerParams(
             collective_id=0, has_side_effects=True, vmem_limit_bytes=60 * 1024 * 1024

time: 214 us -> 186 us (0.87)
  Pallas kernels: 202 us -> 175 us
    pallas_call x1, Pallas kernels: 202 us -> 175 us  [dense(): pl.pallas_call(dense_kernel, out_shape=(jax.ShapeDtypeStruct((tok_rows, w...]
where the time goes in v2:
time: 186 us
  Pallas kernels  175 us (94%)
  local copies, waits for them, and re-layouts  7.83 us (4%)
  other arithmetic  2.7 us (1%)
    pallas_call x1, Pallas kernels, dense(): pl.pallas_call(dense_kernel, out_shape=(jax.ShapeDtypeStruct((tok_rows, w...  175 us
    unnamed x8, local copies, waits for them, and re-layouts  7.83 us

profile of v2, /device:TPU:0, one launch (start us, length us, event | category | flops | bytes accessed | tf_op | source)
XLA Modules:
  0.0 186.0 jit_solution(4588824718771799363)
XLA Ops:
  0.6 0.7 convert_reduce_fusion
  1.3 0.7 divide_bitcast_fusion
  2.0 1.3 select_reduce_fusion.s_hbm
  3.3 174.8 %shard_map.102 = (bf16[128,2048]{1,0:T(8,128)(2,1)}, bf16[2048,384]{1,0:T(8,128)(2,1)}, bf16[2048,384]{1,0:T(8,128)(2,1)}, bf16[384,2048]{1,0:T(8,128)(2,1)}) custom-call(bf16[128,2048]{1,0:T(8,128)(2,1)} %x_hbm.1, bf16[128,2048]{1,0:T(8,128)(2,1)} %g_hbm.1, f32[16,128]{1,0:T(8,128)} %select_reduce_fusion.s_hbm, bf16[2048,384]{1,0:T(8,128)(2,1)} %bitcast.13, ...), custom_call_target="tpu_custom_call" | custom-call | flops 25769803776 | bytes 11010048 | tf_op jit(solution)/shard_map/pallas_call | solution.py:442
  178.1 1.9 %copy.15 = bf16[128,2048]{1,0:T(8,128)(2,1)} copy(bf16[128,2048]{1,0:T(8,128)(2,1)} %get-tuple-element.16) | data formatting | bytes 1048576
  180.0 0.0 copy-start.1
  180.0 2.8 %copy.16 = bf16[1,2048,384]{2,1,0:T(8,128)(2,1)} copy(bf16[1,2048,384]{2,1,0:T(8,128)(2,1)} %bitcast.11) | data formatting | bytes 3145728
  182.9 0.0 copy-done.1
  182.9 0.0 copy-start
  182.9 1.1 copy.17
  184.0 0.8 copy-done
  184.8 1.1 copy.18
Async XLA Ops:
  180.0 2.8 %copy-start.1 = (bf16[2048,384]{1,0:T(8,128)(2,1)S(1)}, bf16[2048,384]{1,0:T(8,128)(2,1)}, u32[]{:S(2)}) copy-start(bf16[2048,384]{1,0:T(8,128)(2,1)} %get-tuple-element.10) | copy-start | bytes 4718596
  182.9 2.0 %copy-start = (bf16[384,2048]{1,0:T(8,128)(2,1)S(1)}, bf16[384,2048]{1,0:T(8,128)(2,1)}, u32[]{:S(2)}) copy-start(bf16[384,2048]{1,0:T(8,128)(2,1)} %get-tuple-element.11) | copy-start | bytes 4718596

commit v3 on v2

--- a/solution.py
+++ b/solution.py
@@ -300,12 +300,12 @@
         def _(j):
             @pl.when(j == 0)
             def _():
-                ahead(p, (2, 0))
-                across(p - 1)
-
                 @pl.loop(0, 2)
                 def _(k):
                     merge(p - 2 + k, jnp.where(k == 0, 1 - y, y))
+
+                ahead(p, (2, 0))
+                across(p - 1)
 
             @pl.when(j == 1)
             def _():

time: 186 us -> 186 us (level)
  no operation moved by 1% of the time
where the time goes in v3:
time: 186 us
  Pallas kernels  174 us (94%)
  local copies, waits for them, and re-layouts  7.83 us (4%)
  other arithmetic  2.7 us (1%)
    pallas_call x1, Pallas kernels, dense(): pl.pallas_call(dense_kernel, out_shape=(jax.ShapeDtypeStruct((tok_rows, w...  174 us
    unnamed x8, local copies, waits for them, and re-layouts  7.83 us

profile of v3, /device:TPU:0, one launch (start us, length us, event | category | flops | bytes accessed | tf_op | source)
XLA Modules:
  0.0 185.6 jit_solution(11020186225284222858)
XLA Ops:
  0.6 0.7 convert_reduce_fusion
  1.3 0.7 divide_bitcast_fusion
  2.0 1.3 select_reduce_fusion.s_hbm
  3.3 174.4 %shard_map.102 = (bf16[128,2048]{1,0:T(8,128)(2,1)}, bf16[2048,384]{1,0:T(8,128)(2,1)}, bf16[2048,384]{1,0:T(8,128)(2,1)}, bf16[384,2048]{1,0:T(8,128)(2,1)}) custom-call(bf16[128,2048]{1,0:T(8,128)(2,1)} %x_hbm.1, bf16[128,2048]{1,0:T(8,128)(2,1)} %g_hbm.1, f32[16,128]{1,0:T(8,128)} %select_reduce_fusion.s_hbm, bf16[2048,384]{1,0:T(8,128)(2,1)} %bitcast.13, ...), custom_call_target="tpu_custom_call" | custom-call | flops 25769803776 | bytes 11010048 | tf_op jit(solution)/shard_map/pallas_call | solution.py:442
  177.7 1.9 %copy.15 = bf16[128,2048]{1,0:T(8,128)(2,1)} copy(bf16[128,2048]{1,0:T(8,128)(2,1)} %get-tuple-element.16) | data formatting | bytes 1048576
  179.6 0.0 copy-start.1
  179.6 2.8 %copy.16 = bf16[1,2048,384]{2,1,0:T(8,128)(2,1)} copy(bf16[1,2048,384]{2,1,0:T(8,128)(2,1)} %bitcast.11) | data formatting | bytes 3145728
  182.4 0.0 copy-done.1
  182.4 0.0 copy-start
  182.4 1.1 copy.17
  183.6 0.8 copy-done
  184.4 1.1 copy.18
Async XLA Ops:
  179.6 2.8 %copy-start.1 = (bf16[2048,384]{1,0:T(8,128)(2,1)S(1)}, bf16[2048,384]{1,0:T(8,128)(2,1)}, u32[]{:S(2)}) copy-start(bf16[2048,384]{1,0:T(8,128)(2,1)} %get-tuple-element.10) | copy-start | bytes 4718596
  182.4 2.0 %copy-start = (bf16[384,2048]{1,0:T(8,128)(2,1)S(1)}, bf16[384,2048]{1,0:T(8,128)(2,1)}, u32[]{:S(2)}) copy-start(bf16[384,2048]{1,0:T(8,128)(2,1)} %get-tuple-element.11) | copy-start | bytes 4718596
